TPU v7x, 256 devices: a whole 4x4x8 slice. The times are simulated.
256 devices in a mesh: col: 32 (over z, x_lo, core), row: 8 (over y, x_hi).
Axes of the slice: x: 4 (x_hi: 2, x_lo: 2; x = x_hi * 2 + x_lo), y: 4, z: 8, core: 2. Of those that a mesh axis runs over, the one named last changes fastest.
Arguments:
- inputs: bfloat16 [1024, 8192], P('col', 'row'), may hold values from -6 to 6
- weight: bfloat16 [8192, 28672], P('row', 'col'), may hold values from -0.0625 to 0.0625
- adapter_down_factors: bfloat16 [16, 16, 8192], P(None, None, 'row'), may hold values from -0.06629126 to 0.06629126
- adapter_up_factors: bfloat16 [16, 16, 28672], P(None, None, 'col'), may hold values from -1.5 to 1.5
- magnitude: float32 [16, 28672], P(None, 'col'), may hold values from 0.5 to 2
- cotangent: bfloat16 [1024, 28672], P('row', 'col'), may hold values from -6 to 6
- tenant: int32 [1024], replicated, may hold values from 0 to 15, as said below
Outputs:
- output: bfloat16 [1024, 28672], P('row', 'col')
- grad_inputs: bfloat16 [1024, 8192], P('col', 'row')
- grad_b: float32 [16, 16, 28672], P(None, None, 'col')
- grad_m: float32 [16, 28672], P(None, 'col')
Inputs may be any that keep to these rules, and one draw needn't show every extreme that they name: `tenant`: constant on each aligned block of 128 tokens; both 0 and 15 occur in every draw.
All inputs are finite; a program needn't handle non-finite values.
Results may differ from a plain program's by a relative error of at most 0.0051.
Values may be sent and summed in bfloat16 or wider, within the bound.
A program may use at most 128 MiB of HBM per device.

v0:
```python
import jax
import jax.numpy as jnp
from jax import lax
from jax.sharding import PartitionSpec as P

BLOCK = 128


HIGH = lax.Precision.HIGHEST
EPS = 1e-06


def direct_norm_terms(weight, adapter_down_factors, adapter_up_factors):
    wf = weight.astype(jnp.float32)

    def single_tenant(pair):
        a_one, b_one = pair
        tile = wf + jnp.einsum(
            "rd,rj->dj", a_one.astype(jnp.float32), b_one.astype(jnp.float32), precision=HIGH
        )
        return jnp.sum(tile * tile, axis=0)

    return lax.map(single_tenant, (adapter_down_factors, adapter_up_factors))


def shards(inputs, weight, adapter_down_factors, adapter_up_factors, magnitude, cotangent, tenant):
    row_count = lax.axis_size("row")
    tenant_number, rank_dimension, width_dimension = adapter_down_factors.shape
    cols = weight.shape[1]
    gathered = lax.all_gather(inputs, "col", axis=0, tiled=True)
    tokens_all = gathered.shape[0]
    nblocks = tokens_all // BLOCK
    block_tenant_index = tenant.reshape(nblocks, BLOCK)[:, 0]
    tenants = jnp.arange(tenant_number, dtype=jnp.int32)
    onehot_tok = (tenant[:, None] == tenants[None, :]).astype(jnp.float32)
    onehot_blk = (tenants[:, None] == block_tenant_index[None, :]).astype(jnp.float32)
    down_factor_blocks = adapter_down_factors[block_tenant_index]
    low_part = jnp.einsum(
        "esc,etc->est",
        down_factor_blocks,
        gathered.reshape(nblocks, BLOCK, width_dimension),
        preferred_element_type=jnp.float32,
    )
    partial_column_norm = direct_norm_terms(weight, adapter_down_factors, adapter_up_factors)
    low_sum, norm_squared_total = lax.psum((low_part, partial_column_norm), "row")
    low_blocks = low_sum.astype(jnp.bfloat16)
    scale = magnitude / jnp.sqrt(norm_squared_total + EPS)
    rows_row = tokens_all // row_count
    row_scale = jnp.dot(onehot_tok, scale, precision=HIGH)
    partial_value = lax.psum_scatter(
        jnp.dot(gathered, weight, preferred_element_type=jnp.float32) * row_scale,
        "row",
        scatter_dimension=0,
        tiled=True,
    )
    blocks_mine = rows_row // BLOCK
    block_start = lax.axis_index("row") * blocks_mine
    local_low_rank = lax.dynamic_slice_in_dim(low_blocks, block_start, blocks_mine, 0)
    local_tenant_index = lax.dynamic_slice_in_dim(block_tenant_index, block_start, blocks_mine, 0)
    onehot_mine = lax.dynamic_slice_in_dim(onehot_blk, block_start, blocks_mine, 1)
    scale_mine = jnp.dot(onehot_mine.T, scale, precision=HIGH)
    adapter = jnp.einsum(
        "dyn,dyz->dnz",
        local_low_rank,
        adapter_up_factors[local_tenant_index],
        preferred_element_type=jnp.float32,
    )
    partial_value = partial_value.reshape(blocks_mine, BLOCK, cols)
    result = partial_value + scale_mine[:, None, :] * adapter
    output = result.reshape(rows_row, cols).astype(jnp.bfloat16)
    grad_all, out_all = (
        lax.all_gather(cotangent, "row", axis=0, tiled=True),
        lax.all_gather(output, "row", axis=0, tiled=True),
    )
    scale_blocks = jnp.dot(onehot_blk.T, scale, precision=HIGH)
    grad_three = grad_all.reshape(nblocks, BLOCK, cols).astype(jnp.float32)
    gradient_scaled = (grad_three * scale_blocks[:, None, :]).astype(jnp.bfloat16)
    per_block = jnp.einsum(
        "brk,bkj->brj", low_blocks, gradient_scaled, preferred_element_type=jnp.float32
    )
    grad_b = jnp.einsum("tb,brj->trj", onehot_blk, per_block, precision=HIGH)
    product = jnp.sum(
        grad_three * out_all.reshape(nblocks, BLOCK, cols).astype(jnp.float32), axis=1
    )
    grad_m = jnp.dot(onehot_blk, product, precision=HIGH) / magnitude
    back_part = jnp.einsum(
        "hty,hxy->htx",
        gradient_scaled,
        adapter_up_factors[block_tenant_index],
        preferred_element_type=jnp.float32,
    )
    back_part = back_part.reshape(tokens_all, rank_dimension)
    grad_flat = gradient_scaled.reshape(tokens_all, cols)
    down_factor_rows = adapter_down_factors[tenant].astype(jnp.float32)
    main = lax.dot_general(
        grad_flat, weight, (((1,), (1,)), ((), ())), preferred_element_type=jnp.float32
    )
    grad_inputs = lax.psum_scatter(
        main + jnp.sum(back_part[:, :, None] * down_factor_rows, axis=1),
        "col",
        scatter_dimension=0,
        tiled=True,
    ).astype(jnp.bfloat16)
    return (output, grad_inputs, grad_b, grad_m)


def solution(mesh):
    return jax.shard_map(
        shards,
        mesh=mesh,
        in_specs=(
            P("col", "row"),
            P("row", "col"),
            P(None, None, "row"),
            P(None, None, "col"),
            P(None, "col"),
            P("row", "col"),
            P(),
        ),
        out_specs=(P("row", "col"), P("col", "row"), P(None, None, "col"), P(None, "col")),
        check_vma=False,
    )
```

profile of v0, /device:TPU:1, one launch (start us, length us, event | category | flops | bytes accessed | tf_op | source)
XLA Modules:
  0.0 486.1 jit_solution(10193722713695075408)
XLA Ops:
  7.2 0.7 all-gather.4.cloned.1.call-update
  8.0 0.8 fusion.16
  8.8 3.5 convert_element_type.40
  12.4 0.6 gather_fusion
  12.9 46.2 %while.11 = (s32[]{:T(128)}, f32[16,896]{1,0:T(8,128)S(1)}, bf16[16,16,1024]{2,1,0:T(8,128)(2,1)S(1)}, bf16[16,16,896]{2,1,0:T(8,128)(2,1)S(1)}, f32[1024,896]{1,0:T(8,128)}, /*index=5*/s32[]{:T(128)}, s32[]{:T(128)}) while((s32[]{:T(128)}, f32[16,896]{1,0:T(8,128)S(1)}, bf16[16,16,1024]{2,1,0:T(8,128)(2,1)S(1)}, ...), condition=%wide.region_2.3_spmd, body=%wide.region_0.2_spmd.sunk | while | flops 32111744 | bytes 3750489 | solution.py:23
  13.0 2.9 multiply_reduce_fusion.3
  15.8 0.1 dynamic_update_slice.5
  16.0 2.7 multiply_reduce_fusion.3
  18.7 0.1 dynamic_update_slice.5
  18.8 2.7 multiply_reduce_fusion.3
  21.6 0.1 dynamic_update_slice.5
  21.7 2.7 multiply_reduce_fusion.3
  24.4 0.1 dynamic_update_slice.5
  24.5 2.8 multiply_reduce_fusion.3
  27.3 0.1 dynamic_update_slice.5
  27.4 2.8 multiply_reduce_fusion.3
  30.2 0.1 dynamic_update_slice.5
  30.4 2.8 multiply_reduce_fusion.3
  33.1 0.1 dynamic_update_slice.5
  33.3 2.8 multiply_reduce_fusion.3
  36.0 0.1 dynamic_update_slice.5
  36.2 2.7 multiply_reduce_fusion.3
  38.9 0.1 dynamic_update_slice.5
  39.0 2.7 multiply_reduce_fusion.3
  41.8 0.1 dynamic_update_slice.5
  41.9 2.7 multiply_reduce_fusion.3
  44.7 0.1 dynamic_update_slice.5
  44.8 2.7 multiply_reduce_fusion.3
  47.6 0.1 dynamic_update_slice.5
  47.7 2.7 multiply_reduce_fusion.3
  50.4 0.1 dynamic_update_slice.5
  50.6 2.8 multiply_reduce_fusion.3
  53.3 0.1 dynamic_update_slice.5
  53.5 2.7 multiply_reduce_fusion.3
  56.2 0.1 dynamic_update_slice.5
  56.3 2.7 multiply_reduce_fusion.3
  59.1 0.1 dynamic_update_slice.5
  59.2 19.6 %all-gather.4.cloned.1.call-done = bf16[1024,1024]{1,0:T(8,128)(2,1)} async-done(((bf16[32,1024]{1,0:T(8,128)(2,1)}), bf16[1024,1024]{1,0:T(8,128)(2,1)}) %all-gather.4.cloned.1.call-update) | async-done | bytes 2097168 | tf_op jit(solution)/shard_map/all_gather | solution.py:30
  78.8 2.2 fusion.29
  81.0 36.2 %all-reduce.2 = (f32[16,896]{1,0:T(8,128)S(1)}, bf16[8,16,128]{2,1,0:T(8,128)(2,1)S(1)}) all-reduce(f32[16,896]{1,0:T(8,128)S(1)} %get-tuple-element.31, f32[8,16,128]{2,1,0:T(8,128)S(1)} %fusion.29), channel_id=1, replica_groups=mesh['col'=32,'row'=8] {'row'}, use_global_device_ids=true, to_apply=%region_3.4 | all-reduce | flops 30720 | bytes 212992 | tf_op jit(solution)/shard_map/psum | solution.py:45
  117.3 3.9 fusion.28
  121.2 3.6 convolution_multiply_fusion
  124.9 0.7 all-gather.6.cloned.1.call-update
  125.6 0.5 constant_dynamic-slice_fusion
  128.2 0.2 convolution_reduce_fusion
  128.3 84.2 %reduce-scatter.3.cloned.1.call-done = f32[128,896]{1,0:T(8,128)} async-done(((f32[1024,896]{1,0:T(8,128)}), f32[128,896]{1,0:T(8,128)}) %reduce-scatter.3.cloned.1.call-update) | async-done | bytes 458768 | tf_op jit(solution)/shard_map/reduce_scatter | solution.py:50
  212.6 2.0 fusion.8
  214.6 0.6 gather_fusion.1
  215.2 18.5 %gather_fusion.2 = bf16[1024,16,1024]{2,1,0:T(8,128)(2,1)} fusion(bf16[16,16,1024]{2,1,0:T(8,128)(2,1)S(1)} %get-tuple-element.129, s32[1024]{0:T(1024)S(1)} %fusion.17), kind=kCustom, calls=%fused_computation.2 | custom fusion | bytes 67112960 | tf_op jit(solution)/shard_map/gather | solution.py:94
  233.7 0.2 fusion.21
  233.8 38.0 %all-gather.6.cloned.1.call-done = bf16[1024,896]{1,0:T(8,128)(2,1)} async-done(((bf16[128,896]{1,0:T(8,128)(2,1)}), bf16[1024,896]{1,0:T(8,128)(2,1)}) %all-gather.6.cloned.1.call-update) | async-done | bytes 1835024 | tf_op jit(solution)/shard_map/all_gather | solution.py:72
  271.8 3.2 fusion.6
  275.1 54.8 %all-gather.8.cloned.1.call-done = bf16[1024,896]{1,0:T(8,128)(2,1)} async-done(((bf16[128,896]{1,0:T(8,128)(2,1)}), bf16[1024,896]{1,0:T(8,128)(2,1)}) %all-gather.8.cloned.1.call-update) | async-done | bytes 1835024 | tf_op jit(solution)/shard_map/all_gather | solution.py:73
  329.8 2.0 fusion.5
  331.9 1.8 copy-done.1
  333.6 0.6 fusion.10
  334.3 18.5 %multiply_reduce_fusion.1 = f32[1024,1024]{1,0:T(8,128)} fusion(bf16[1024,16,1024]{2,1,0:T(8,128)(2,1)} %gather_fusion.2, f32[1024,16]{1,0:T(8,128)S(1)} %bitcast.45), kind=kLoop, calls=%fused_computation.9 | loop fusion | flops 49283072 | bytes 37814272 | tf_op jit(solution)/shard_map/reduce_sum | solution.py:99
  352.8 7.1 %convolution_add_fusion = f32[1024,1024]{1,0:T(8,128)} fusion(f32[1024,1024]{1,0:T(8,128)} %multiply_reduce_fusion.1, bf16[1024,896]{1,0:T(8,128)(2,1)S(1)} %copy-done.3, bf16[1024,896]{1,0:T(8,128)(2,1)} %param.10), kind=kOutput, calls=%fused_computation.16 | convolution fusion | flops 1880096768 | bytes 12058624 | tf_op jit(solution)/shard_map/dot_general | solution.py:95
  360.0 2.4 fusion.9
  362.4 0.6 fusion.11
  363.1 1.2 copy.18
  364.3 0.9 convolution_divide_fusion
  365.2 112.8 %reduce-scatter.5.cloned.1.call-done = f32[32,1024]{1,0:T(8,128)} async-done(((f32[1024,1024]{1,0:T(8,128)}), f32[32,1024]{1,0:T(8,128)}) %reduce-scatter.5.cloned.1.call-update) | async-done | bytes 131088 | tf_op jit(solution)/shard_map/reduce_scatter | solution.py:98
  478.0 1.5 convert_element_type.49
  (43 shorter events, 0.4 us)
Async XLA Ops:
  7.2 5.2 %copy-start = (bf16[16,16,1024]{2,1,0:T(8,128)(2,1)S(1)}, bf16[16,16,1024]{2,1,0:T(8,128)(2,1)}, u32[]{:S(2)}) copy-start(bf16[16,16,1024]{2,1,0:T(8,128)(2,1)} %param.11) | copy-start | bytes 1572868
  7.2 5.7 %copy-start.6 = (bf16[16,16,896]{2,1,0:T(8,128)(2,1)S(1)}, bf16[16,16,896]{2,1,0:T(8,128)(2,1)}, u32[]{:S(2)}) copy-start(bf16[16,16,896]{2,1,0:T(8,128)(2,1)} %param.12) | copy-start | bytes 1376260
  7.2 71.6 %all-gather.4.cloned.1.call-start = ((), (), s32[]{:S(2)}) async-start(), calls=%async_computation.2 | async-start | bytes 2162688 | tf_op jit(solution)/shard_map/all_gather | solution.py:30
  7.9 204.6 %reduce-scatter.3.cloned.1.call-start = ((), (), s32[]{:S(2)}) async-start(), calls=%async_computation.3 | async-start | bytes 4128768 | tf_op jit(solution)/shard_map/reduce_scatter | solution.py:50
  12.9 104.3 %copy-start.4 = (bf16[1024,896]{1,0:T(8,128)(2,1)S(1)}, bf16[1024,896]{1,0:T(8,128)(2,1)}, u32[]{:S(2)}) copy-start(bf16[1024,896]{1,0:T(8,128)(2,1)} %param.10) | copy-start | bytes 5505028
  117.2 4.0 copy-start.5
  117.3 4.0 copy-start.7
  124.8 147.0 %all-gather.6.cloned.1.call-start = ((), (), s32[]{:S(2)}) async-start(), calls=%async_computation.4 | async-start | bytes 2064384 | tf_op jit(solution)/shard_map/all_gather | solution.py:72
  125.6 204.3 %all-gather.8.cloned.1.call-start = ((), (), s32[]{:S(2)}) async-start(), calls=%async_computation.6 | async-start | bytes 2064384 | tf_op jit(solution)/shard_map/all_gather | solution.py:73
  214.5 263.4 %reduce-scatter.5.cloned.1.call-start = ((), (), s32[]{:S(2)}) async-start(), calls=%async_computation.5 | async-start | bytes 4325376 | tf_op jit(solution)/shard_map/reduce_scatter | solution.py:98
  271.8 58.0 %copy-start.2 = (bf16[1024,896]{1,0:T(8,128)(2,1)S(1)}, bf16[1024,896]{1,0:T(8,128)(2,1)}, u32[]{:S(2)}) copy-start(bf16[1024,896]{1,0:T(8,128)(2,1)} %all-gather.6.cloned.1.call-done) | copy-start | bytes 5505028
  331.9 1.8 copy-start.1
  334.3 18.6 %copy-start.3 = (bf16[1024,896]{1,0:T(8,128)(2,1)S(1)}, bf16[1024,896]{1,0:T(8,128)(2,1)}, u32[]{:S(2)}) copy-start(bf16[1024,896]{1,0:T(8,128)(2,1)} %fusion.6) | copy-start | bytes 5505028
Sparse Core Ops, SparseCore 0:
  9.9 68.8 all-gather.3
  125.0 87.5 reduce-scatter.2
  215.2 56.6 all-gather.5
  274.8 54.9 all-gather.7
  360.1 117.8 reduce-scatter.4
where the time goes:
time: 490 us; the launch traced here: 486 us
  waiting for transfers between devices  311 us (63%)
  matrix products  67.8 us (14%)
  blocking collectives  36.2 us (7%)
  other arithmetic  29.8 us (6%)
  local copies, waits for them, and re-layouts  24.8 us (5%)
  between operations  15.9 us (3%)
    reduce_scatter x1, waiting for transfers between devices, shards(): lax.psum_scatter(main + jnp.sum(back_part[:, :, None] * down_factor_rows,...  113 us
    reduce_scatter x1, waiting for transfers between devices, shards(): lax.psum_scatter(jnp.dot(gathered, weight, preferred_element_type=jnp.flo...  84.2 us
    all_gather x1, waiting for transfers between devices, shards(): lax.all_gather(output, 'row', axis=0, tiled=True)  54.8 us
    dot_general x16, matrix products, single_tenant(): jnp.einsum('rd,rj->dj', a_one.astype(jnp.float32), b_one.astype(jnp.float...  44 us
    all_gather x1, waiting for transfers between devices, shards(): lax.all_gather(cotangent, 'row', axis=0, tiled=True)  38 us
    psum x1, blocking collectives, shards(): lax.psum((low_part, partial_column_norm), 'row')  36.2 us
    all_gather x1, waiting for transfers between devices, shards(): gathered = lax.all_gather(inputs, 'col', axis=0, tiled=True)  19.6 us
    reduce_sum x1, other arithmetic, shards(): jnp.sum(back_part[:, :, None] * down_factor_rows, axis=1)  18.5 us
  transfers between devices with their start and end apart: 5, of which 5 were waited for; matrix products, arithmetic and copies ran while one was open for 17% of the time, Pallas kernels for 0%

commit v1 on v0

v1 whole, which is shorter than its diff:
```python
import functools

import jax
import jax.numpy as jnp
from jax import lax
from jax.experimental import pallas as pl
from jax.experimental.pallas import tpu as pltpu
from jax.sharding import PartitionSpec as P

EPS = 1e-06
MESH = pl.DeviceIdType.MESH
BF = jnp.bfloat16
F32 = jnp.float32

NZ, NY, NR = 8, 4, 8
FIRST_BACK = 6
STEPS = FIRST_BACK + NZ + 2


def mm(a, b):
    return jnp.dot(a, b, preferred_element_type=F32)


def mm_nt(a, b):
    return lax.dot_general(a, b, (((1,), (1,)), ((), ())), preferred_element_type=F32)


def lane_tiles(width):
    return [(n, min(n + 256, width)) for n in range(0, width, 256)]


def kernel(
    ten, x_in, w_in, a_in, u_in, mag, c_in,
    out_ref, gi_ref, gb_ref, gm_ref,
    w_v, a_v, u_v, xb, cb, sgb, gb_v,
    nsend, nrecv, sbuf,
    lsend, lrecv, lowb,
    pf, ps, rb, xsb, xrb,
    gp, csend, crecv, e_own, xsend, xrecv, zsend, zrecv,
    gms,
    loc_sem, gb_sem,
    zs, zr, x2s, x2r, c3s, c3r,
    cs, cr,
    n1s, n1r, n2s, n2r, l1s, l1r, l2s, l2r, gs, gr,
    pss, prs, pxs, pxr,
    bcs, bcr, bxs, bxr, bzs, bzr,
):
    col = lax.axis_index("col")
    row = lax.axis_index("row")
    z, xl, c = col // 4, (col // 2) % 2, col % 2
    y, xh = row // 2, row % 2
    cols = w_v.shape[1]
    width = w_v.shape[0]

    def at_col(zz, xx, cc):
        return {"col": (zz * 2 + xx) * 2 + cc, "row": row}

    def at_row(rr):
        return {"col": col, "row": rr}

    core_mate = at_col(z, xl, 1 - c)
    x_mate = at_col(z, 1 - xl, c)
    y_up = at_row(((y + 1) % NY) * 2 + xh)
    y_down = at_row(((y + NY - 1) % NY) * 2 + xh)
    far_mate = at_row(y * 2 + 1 - xh)

    def rcopy(src, dst, ssem, rsem, dev):
        return pltpu.make_async_remote_copy(
            src_ref=src, dst_ref=dst, send_sem=ssem, recv_sem=rsem,
            device_id=dev, device_id_type=MESH,
        )

    def got(dst, rsem):
        rcopy(dst, dst, rsem, rsem, core_mate).wait_recv()

    def sent(src, ssem):
        rcopy(src, src, ssem, ssem, core_mate).wait_send()

    def block_tenant(b):
        return ten[b * 128]

    loads = [
        pltpu.make_async_copy(x_in, xb.at[z, c, xl], loc_sem.at[0]),
        pltpu.make_async_copy(w_in, w_v, loc_sem.at[1]),
        pltpu.make_async_copy(a_in, a_v, loc_sem.at[2]),
        pltpu.make_async_copy(u_in, u_v, loc_sem.at[3]),
        pltpu.make_async_copy(c_in, cb.at[row], loc_sem.at[4]),
    ]
    for one in loads:
        one.start()

    barrier = pltpu.get_barrier_semaphore()
    for o in range(1, NZ):
        pl.semaphore_signal(barrier, inc=1, device_id=at_col((z + o) % NZ, xl, c), device_id_type=MESH)
    for o in range(1, NR):
        pl.semaphore_signal(barrier, inc=1, device_id=at_row((row + o) % NR), device_id_type=MESH)
    pl.semaphore_signal(barrier, inc=1, device_id=x_mate, device_id_type=MESH)
    pl.semaphore_signal(barrier, inc=1, device_id=core_mate, device_id_type=MESH)
    pl.semaphore_wait(barrier, (NZ - 1) + (NR - 1) + 2)

    def zcopy(o):
        return rcopy(x_in, xb.at[z, c, xl], zs.at[o], zr.at[z], at_col((z + o) % NZ, xl, c))

    for o in (1, 7, 2, 6, 3, 5, 4):
        zcopy(o).start()

    def cot_copy(i, src, b, dev):
        return rcopy(src, cb.at[b], cs.at[i], cr.at[b], dev)

    b_far = y * 2 + 1 - xh
    b_dn = ((y + NY - 1) % NY) * 2 + xh
    b_upfar = ((y + 1) % NY) * 2 + 1 - xh
    cot_sends = [
        cot_copy(0, c_in, row, far_mate),
        cot_copy(1, c_in, row, y_up),
        cot_copy(2, c_in, row, y_down),
        cot_copy(3, cb.at[b_far], b_far, y_up),
        cot_copy(4, cb.at[b_far], b_far, y_down),
        cot_copy(5, cb.at[b_dn], b_dn, y_up),
        cot_copy(6, cb.at[b_upfar], b_upfar, y_down),
    ]
    for one in cot_sends[:3]:
        one.start()

    for one in loads:
        one.wait()
    a_all = a_v[...].reshape(NR * 2 * 16, width)
    aat = mm_nt(a_all, a_all)
    same = lax.broadcasted_iota(jnp.int32, aat.shape, 0) // 16 == lax.broadcasted_iota(jnp.int32, aat.shape, 1) // 16
    gram = jnp.where(same, aat, 0.0)
    gram_hi = gram.astype(BF)
    gram_lo = (gram - gram_hi.astype(F32)).astype(BF)
    for n0, n1 in lane_tiles(cols):
        wt = w_v[:, n0:n1]
        ut = u_v[:, :, n0:n1].reshape(256, n1 - n0)
        val = 2.0 * mm(a_all, wt) + (mm(gram_hi, ut) + mm(gram_lo, ut))
        quad = jnp.sum((ut.astype(F32) * val).reshape(16, 16, n1 - n0), axis=1)
        wf = wt.astype(F32)
        wsq = jnp.sum(jnp.sum((wf * wf).reshape(width // 8, 8, n1 - n0), axis=0), axis=0, keepdims=True)
        nsq = quad + wsq
        for r in range(NR):
            nsend[r, :, n0:n1] = nsq[2 * r:2 * r + 2]
    nrecv[row] = nsend[row]

    def n1copy(o):
        r = (row + o) % NR
        return rcopy(nsend.at[r], nrecv.at[row], n1s.at[o], n1r.at[row], at_row(r))

    for o in range(1, NR):
        n1copy(o).start()

    def n2copy(o):
        r = (row + o) % NR
        return rcopy(sbuf.at[row], sbuf.at[row], n2s.at[o], n2r.at[row], at_row(r))

    def l1copy(r):
        return rcopy(lsend.at[r], lrecv.at[row], l1s.at[r], l1r.at[row], at_row(r))

    def l2copy(o):
        r = (row + o) % NR
        return rcopy(lowb.at[row], lowb.at[row], l2s.at[o], l2r.at[row], at_row(r))

    def z_of(k):
        return (z + NZ + jnp.where(k % 2 == 1, (k + 1) // 2, -(k // 2))) % NZ

    def b_of(q):
        dy = jnp.where(q >= 6, 2, jnp.where(q % 3 == 2, 3, q % 3))
        dx = jnp.where(q >= 6, q - 6, q // 3)
        return ((y + dy) % NY) * 2 + (xh + dx) % 2

    def x2copy(zz):
        return rcopy(xb.at[zz, c, xl], xb.at[zz, c, xl], x2s.at[zz], x2r.at[zz], x_mate)

    def c3copy(zz):
        return rcopy(xb.at[zz, c], xb.at[zz, c], c3s.at[zz], c3r.at[zz], core_mate)

    def pre_slot(dy, xx):
        return jnp.where(dy == 2, 4 + xx, jnp.where(dy == 1, xx, 2 + xx))

    def pre_copy(dy, xx):
        slot = pre_slot(dy, xx)
        up = (dy == 1) | ((dy == 2) & (xx == 0))
        yy = jnp.where(up, (y + 1) % NY, (y + NY - 1) % NY)
        return rcopy(ps.at[dy, xx], rb.at[slot], pss.at[slot], prs.at[slot], at_row(yy * 2 + xh))

    far_copy = rcopy(xsb, xrb, pxs, pxr, far_mate)

    def bccopy(b):
        return rcopy(csend.at[b], crecv.at[b], bcs.at[b], bcr.at[b], core_mate)

    def bxcopy(b):
        return rcopy(xsend.at[b], xrecv.at[b], bxs.at[b], bxr.at[b], x_mate)

    def bzcopy(b):
        return rcopy(zsend.at[b], zrecv.at[z], bzs.at[b], bzr.at[z], at_col(b, xl, c))

    def forward_block(zz):
        xs = jnp.concatenate([xb[zz, 0, 0], xb[zz, 1, 0], xb[zz, 0, 1], xb[zz, 1, 1]], axis=0)
        dy = (zz // 2 + NY - y) % NY
        xx = zz % 2
        for n0, n1 in lane_tiles(cols):
            part = mm(xs, w_v[:, n0:n1])
            pf[dy, xx, :, n0:n1] = part
            ps[dy, xx, :, n0:n1] = part.astype(BF)
        low = mm_nt(a_v[block_tenant(zz)], xs)
        lsend[zz] = low

        @pl.when((dy == 2) | ((dy == 1) & (xx == 1)) | ((dy == 3) & (xx == 0)))
        def _():
            pre_copy(dy, xx).start()

        @pl.when(zz != row)
        def _():
            l1copy(zz).start()

        @pl.when(zz == row)
        def _():
            lrecv[row] = low

    def token_scale(b):
        t = block_tenant(b)
        s = sbuf[...]
        number = lax.broadcasted_iota(jnp.int32, s.shape, 0) * 2 + lax.broadcasted_iota(jnp.int32, s.shape, 1)
        return jnp.sum(jnp.sum(jnp.where(number == t, s, 0.0), axis=0), axis=0, keepdims=True)

    def backward_block(b):
        t = block_tenant(b)
        sg = (cb[b].astype(F32) * token_scale(b)).astype(BF)
        sgb[b] = sg
        u = u_v[t]
        a = a_v[t]
        back = mm_nt(sg, jnp.concatenate([u, u], axis=0))
        hi = back.astype(BF).astype(F32)
        lane = lax.broadcasted_iota(jnp.int32, back.shape, 1)
        both = jnp.where(lane < 16, hi, back - hi).astype(BF)
        a2 = jnp.concatenate([a, a], axis=0)
        for n0, n1 in lane_tiles(width):
            part = mm_nt(sg, w_v[n0:n1, :]) + mm(both, a2[:, n0:n1])
            gp[b, :, :, :, n0:n1] = part.reshape(2, 2, 32, n1 - n0)
        csend[b] = gp[b, :, 1 - c].astype(BF)
        bccopy(b).start()

    def step(s, carry):
        @pl.when(s < NZ)
        def _():
            zz = z_of(s)

            @pl.when(s > 0)
            def _():
                got(xb.at[zz, c, xl], zr.at[zz])

            x2copy(zz).start()

        @pl.when((s >= 1) & (s < NZ + 1))
        def _():
            zz = z_of(s - 1)
            got(xb.at[zz, c, 1 - xl], x2r.at[zz])
            c3copy(zz).start()

        @pl.when(s == 2)
        def _():
            got(cb.at[b_far], cr.at[b_far])
            cot_sends[3].start()
            cot_sends[4].start()

        @pl.when(s == 4)
        def _():
            got(cb.at[b_dn], cr.at[b_dn])
            cot_sends[5].start()
            for o in range(1, NR):
                r = (row + o) % NR
                got(nrecv.at[r], n1r.at[r])
            total = jnp.sum(nrecv[...], axis=0)
            m = mag[...]
            number = lax.broadcasted_iota(jnp.int32, m.shape, 0)
            mine = jnp.concatenate(
                [jnp.sum(jnp.where(number == 2 * row + i, m, 0.0), axis=0, keepdims=True) for i in range(2)], axis=0
            )
            sbuf[row] = mine / jnp.sqrt(total + EPS)
            for o in range(1, NR):
                n2copy(o).start()

        @pl.when((s >= 2) & (s < NZ + 2))
        def _():
            zz = z_of(s - 2)
            got(xb.at[zz, 1 - c], c3r.at[zz])
            forward_block(zz)

        @pl.when(s == FIRST_BACK)
        def _():
            for o in range(1, NR):
                r = (row + o) % NR
                got(sbuf.at[r], n2r.at[r])
            got(cb.at[b_upfar], cr.at[b_upfar])
            cot_sends[6].start()

        @pl.when(s == NZ + 2)
        def _():
            got(rb.at[4], prs.at[4])
            ps[1, 0] = (pf[1, 0] + rb[4].astype(F32)).astype(BF)
            pre_copy(1, 0).start()
            got(rb.at[5], prs.at[5])
            ps[3, 1] = (pf[3, 1] + rb[5].astype(F32)).astype(BF)
            pre_copy(3, 1).start()

        @pl.when(s == NZ + 4)
        def _():
            for o in range(1, NR):
                r = (row + o) % NR
                got(lrecv.at[r], l1r.at[r])
            lowb[row] = jnp.sum(lrecv[...], axis=0).astype(BF)
            for o in range(1, NR):
                l2copy(o).start()

        @pl.when((s >= FIRST_BACK) & (s < FIRST_BACK + NR))
        def _():
            q = s - FIRST_BACK
            b = b_of(q)

            @pl.when((q == 1) | (q >= 5))
            def _():
                got(cb.at[b], cr.at[b])

            backward_block(b)

        @pl.when((s >= FIRST_BACK + 1) & (s < FIRST_BACK + 1 + NR))
        def _():
            b = b_of(s - FIRST_BACK - 1)
            got(crecv.at[b], bcr.at[b])
            xsend[b] = (gp[b, 1 - xl, c] + crecv[b, 1 - xl].astype(F32)).astype(BF)
            bxcopy(b).start()
            e_own[b] = gp[b, xl, c] + crecv[b, xl].astype(F32)

        @pl.when(s >= FIRST_BACK + 2)
        def _():
            b = b_of(s - FIRST_BACK - 2)
            got(xrecv.at[b], bxr.at[b])
            both = e_own[b] + xrecv[b].astype(F32)
            zsend[b] = both.astype(BF)

            @pl.when(b != z)
            def _():
                bzcopy(b).start()

            @pl.when(b == z)
            def _():
                e_own[b] = both

        return carry

    lax.fori_loop(0, STEPS, step, 0)

    for slot in range(4):
        got(rb.at[slot], prs.at[slot])
    xx = 1 - xh
    xsb[...] = (pf[0, xx] + rb[xx].astype(F32) + rb[2 + xx].astype(F32)).astype(BF)
    far_copy.start()

    for o in range(1, NR):
        r = (row + o) % NR
        got(lowb.at[r], l2r.at[r])
    pieces = []
    for b in range(NR):
        wide = jnp.concatenate([lowb[b].astype(F32)] * 16, axis=0)
        number = lax.broadcasted_iota(jnp.int32, wide.shape, 0) // 16
        pieces.append(jnp.where(number == block_tenant(b), wide, 0.0).astype(BF))
    low_wide = jnp.concatenate(pieces, axis=1)
    for n0, n1 in lane_tiles(cols):
        sg = sgb[:, :, n0:n1].reshape(NR * 128, n1 - n0)
        gb_v[:, :, n0:n1] = mm(low_wide, sg).reshape(16, 16, n1 - n0)
    gb_out = pltpu.make_async_copy(gb_v, gb_ref, gb_sem)
    gb_out.start()

    got(xrb, pxr)
    u_mine = u_v[block_tenant(row)]
    low_mine = lowb[row].astype(F32).T.astype(BF)
    scale_mine = token_scale(row)
    for n0, n1 in lane_tiles(cols):
        pre = pf[0, xh, :, n0:n1] + rb[xh, :, n0:n1].astype(F32) + rb[2 + xh, :, n0:n1].astype(F32)
        pre = pre + xrb[:, n0:n1].astype(F32) + mm(low_mine, u_mine[:, n0:n1])
        result = (pre * scale_mine[:, n0:n1]).astype(BF)
        out_ref[:, n0:n1] = result
        product = cb[row, :, n0:n1].astype(F32) * result.astype(F32)
        gms[row, :, n0:n1] = jnp.sum(product, axis=0, keepdims=True)

    def gcopy(o):
        r = (row + o) % NR
        return rcopy(gms.at[row], gms.at[row], gs.at[o], gr.at[row], at_row(r))

    for o in range(1, NR):
        gcopy(o).start()

    for o in range(1, NZ):
        zz = (z + o) % NZ
        got(zrecv.at[zz], bzr.at[zz])
    total = e_own[z]
    for o in range(1, NZ):
        total = total + zrecv[(z + o) % NZ].astype(F32)
    gi_ref[...] = total.astype(BF)

    for o in range(1, NR):
        r = (row + o) % NR
        got(gms.at[r], gr.at[r])
    m = mag[...]
    number = lax.broadcasted_iota(jnp.int32, m.shape, 0)
    acc = jnp.zeros_like(m)
    for b in range(NR):
        acc = acc + jnp.where(number == block_tenant(b), gms[b], 0.0)
    gm_ref[...] = acc / m

    gb_out.wait()
    for o in range(1, NZ):
        sent(x_in, zs.at[o])
        sent(nsend.at[0], n1s.at[o])
        sent(sbuf.at[0], n2s.at[o])
        sent(lowb.at[0], l2s.at[o])
        sent(gms.at[0], gs.at[o])
    for k in range(NZ):
        sent(xb.at[k, 0, 0], x2s.at[k])
        sent(xb.at[k, 0], c3s.at[k])
        sent(csend.at[k], bcs.at[k])
        sent(xsend.at[k], bxs.at[k])

        @pl.when(k != z)
        def _():
            sent(zsend.at[k], bzs.at[k])

        @pl.when(k != row)
        def _():
            sent(lsend.at[k], l1s.at[k])
    for i in range(7):
        sent(c_in, cs.at[i])
    for i in range(6):
        sent(rb.at[i], pss.at[i])
    sent(xsb, pxs)


def shards(inputs, weight, adapter_down_factors, adapter_up_factors, magnitude, cotangent, tenant):
    width, cols = weight.shape
    tokens, rows = inputs.shape[0], cotangent.shape[0]
    any_, vmem = pl.BlockSpec(memory_space=pl.ANY), pl.BlockSpec(memory_space=pltpu.VMEM)
    dma = pltpu.SemaphoreType.DMA
    V = pltpu.VMEM
    return pl.pallas_call(
        kernel,
        out_shape=(
            jax.ShapeDtypeStruct((rows, cols), BF),
            jax.ShapeDtypeStruct((tokens, width), BF),
            jax.ShapeDtypeStruct((16, 16, cols), F32),
            jax.ShapeDtypeStruct((16, cols), F32),
        ),
        in_specs=[pl.BlockSpec(memory_space=pltpu.SMEM), any_, any_, any_, any_, vmem, any_],
        out_specs=(vmem, vmem, any_, vmem),
        scratch_shapes=[
            V((width, cols), BF), V((16, 16, width), BF), V((16, 16, cols), BF),
            V((NZ, 2, 2, tokens, width), BF), V((NR, rows, cols), BF), V((NR, rows, cols), BF),
            V((16, 16, cols), F32),
            V((NR, 2, cols), F32), V((NR, 2, cols), F32), V((NR, 2, cols), F32),
            V((NR, 16, rows), F32), V((NR, 16, rows), F32), V((NR, 16, rows), BF),
            V((NY, 2, rows, cols), F32), V((NY, 2, rows, cols), BF), V((6, rows, cols), BF),
            V((rows, cols), BF), V((rows, cols), BF),
            V((NR, 2, 2, tokens, width), F32), V((NR, 2, tokens, width), BF), V((NR, 2, tokens, width), BF),
            V((NR, tokens, width), F32),
            V((NR, tokens, width), BF), V((NR, tokens, width), BF),
            V((NR, tokens, width), BF), V((NR, tokens, width), BF),
            V((NR, 1, cols), F32),
            dma((5,)), dma,
            dma((8,)), dma((8,)), dma((8,)), dma((8,)), dma((8,)), dma((8,)),
            dma((7,)), dma((8,)),
            dma((8,)), dma((8,)), dma((8,)), dma((8,)), dma((8,)), dma((8,)), dma((8,)), dma((8,)), dma((8,)), dma((8,)),
            dma((6,)), dma((6,)), dma, dma,
            dma((8,)), dma((8,)), dma((8,)), dma((8,)), dma((8,)), dma((8,)),
        ],
        compiler_params=pltpu.CompilerParams(
            collective_id=0, has_side_effects=True, vmem_limit_bytes=56 << 20
        ),
        cost_estimate=pl.CostEstimate(flops=6 * 10**9, bytes_accessed=8 * 10**6, transcendentals=10**5),
        name="adapter_step",
    )(tenant, inputs, weight, adapter_down_factors, adapter_up_factors, magnitude, cotangent)


def solution(mesh):
    return jax.shard_map(
        shards,
        mesh=mesh,
        in_specs=(
            P("col", "row"),
            P("row", "col"),
            P(None, None, "row"),
            P(None, None, "col"),
            P(None, "col"),
            P("row", "col"),
            P(),
        ),
        out_specs=(P("row", "col"), P("col", "row"), P(None, None, "col"), P(None, "col")),
        check_vma=False,
    )
```

time: 490 us -> 92.9 us (0.19)
  the two profiles are of different devices: /device:TPU:1 before, /device:TPU:32 now
where the time goes in v1:
time: 92.9 us; the launch traced here: 92.7 us
  Pallas kernels  86.1 us (93%)
  local copies, waits for them, and re-layouts  5.92 us (6%)
    pallas_call x1, Pallas kernels, shards(): pl.pallas_call(kernel, out_shape=(jax.ShapeDtypeStruct((rows, cols), BF),...  86.1 us
    unnamed x6, local copies, waits for them, and re-layouts  5.92 us

profile of v1, /device:TPU:32, one launch (start us, length us, event | category | flops | bytes accessed | tf_op | source)
XLA Modules:
  0.0 92.7 jit_solution(15995556836422844950)
XLA Ops:
  0.6 86.1 %adapter_step.1 = (bf16[128,896]{1,0:T(8,128)(2,1)}, bf16[32,1024]{1,0:T(8,128)(2,1)}, f32[16,16,896]{2,1,0:T(8,128)}, f32[16,896]{1,0:T(8,128)}) custom-call(s32[1024]{0:T(1024)} %ten.1, bf16[32,1024]{1,0:T(8,128)(2,1)} %x_in.1, bf16[1024,896]{1,0:T(8,128)(2,1)} %w_in.1, bf16[16,16,1024]{2,1,0:T(8,128)(2,1)} %a_in.1, bf16[16,16,896]{2,1,0:T(8,128)(2,1)} %u_in.1, ...), custom_call_target="tpu_custom_call" | custom-call | flops 6000000000 | bytes 8000000 | tf_op jit(solution)/shard_map/adapter_step/pallas_call | solution.py:444
  86.7 0.0 copy-start
  86.8 1.7 %copy.15 = bf16[128,896]{1,0:T(8,128)(2,1)} copy(bf16[128,896]{1,0:T(8,128)(2,1)} %get-tuple-element.8) | data formatting | bytes 458752
  88.4 1.5 %copy.16 = bf16[32,1024]{1,0:T(8,128)(2,1)} copy(bf16[32,1024]{1,0:T(8,128)(2,1)} %get-tuple-element.9) | data formatting | bytes 131072
  89.9 2.2 %copy.17 = f32[16,16,896]{2,1,0:T(8,128)} copy(f32[16,16,896]{2,1,0:T(8,128)} %get-tuple-element.10) | data formatting | bytes 1835008
  92.0 0.0 copy-done
  92.0 0.6 copy.18
Async XLA Ops:
  86.7 5.3 %copy-start = (f32[16,896]{1,0:T(8,128)S(1)}, f32[16,896]{1,0:T(8,128)}, u32[]{:S(2)}) copy-start(f32[16,896]{1,0:T(8,128)} %get-tuple-element.11) | copy-start | bytes 172036

commit v2 on v1

--- a/solution.py
+++ b/solution.py
@@ -13,8 +13,11 @@
 F32 = jnp.float32
 
 NZ, NY, NR = 8, 4, 8
-FIRST_BACK = 6
-STEPS = FIRST_BACK + NZ + 2
+AT_FAR, AT_DOWN, AT_UPFAR = 2, 2, 6
+AT_NORM, AT_SCALE, AT_VIA, AT_LOW = 1, 5, 13, 13
+FIRST_BACK, LAG_X, LAG_Z = 5, 2, 4
+FAR_OFF = 5
+STEPS = FIRST_BACK + NZ + LAG_Z
 
 
 def mm(a, b):
@@ -35,14 +38,14 @@
     w_v, a_v, u_v, xb, cb, sgb, gb_v,
     nsend, nrecv, sbuf,
     lsend, lrecv, lowb,
-    pf, ps, rb, xsb, xrb,
+    pf, ps, rb, xsb, xrb, rd,
     gp, csend, crecv, e_own, xsend, xrecv, zsend, zrecv,
     gms,
     loc_sem, gb_sem,
     zs, zr, x2s, x2r, c3s, c3r,
     cs, cr,
     n1s, n1r, n2s, n2r, l1s, l1r, l2s, l2r, gs, gr,
-    pss, prs, pxs, pxr,
+    pss, prs, pxs, pxr, ds, dr,
     bcs, bcr, bxs, bxr, bzs, bzr,
 ):
     col = lax.axis_index("col")
@@ -98,11 +101,36 @@
     pl.semaphore_signal(barrier, inc=1, device_id=core_mate, device_id_type=MESH)
     pl.semaphore_wait(barrier, (NZ - 1) + (NR - 1) + 2)
 
-    def zcopy(o):
-        return rcopy(x_in, xb.at[z, c, xl], zs.at[o], zr.at[z], at_col((z + o) % NZ, xl, c))
-
-    for o in (1, 7, 2, 6, 3, 5, 4):
-        zcopy(o).start()
+    z_up, z_down = at_col((z + 1) % NZ, xl, c), at_col((z + NZ - 1) % NZ, xl, c)
+
+    def ring_place(slab, h, way):
+        if h < 4:
+            return xb.at[slab, c, xl], zr.at[slab, 0]
+        return xb.at[slab, c, xl, pl.ds(16 * way, 16)], zr.at[slab, way]
+
+    def ring(way, h):
+        slab = (z + NZ - h) % NZ if way == 0 else (z + h) % NZ
+        place, arrived = ring_place(slab, h + 1, way)
+        src = x_in if h == 0 else place
+        return rcopy(src, place, zs.at[way, h], arrived, z_up if way == 0 else z_down)
+
+    def ring_got(way, h):
+        slab = (z + NZ - h) % NZ if way == 0 else (z + h) % NZ
+        got(*ring_place(slab, h, way))
+
+    def x2copy(zz, src=None):
+        place = xb.at[zz, c, xl]
+        return rcopy(place if src is None else src, place, x2s.at[zz], x2r.at[zz], x_mate)
+
+    def x2_got(zz):
+        got(xb.at[zz, c, 1 - xl], x2r.at[zz])
+
+    ring(0, 0).start()
+    ring(1, 0).start()
+    x2copy(z, x_in).start()
+
+    def c3copy(zz):
+        return rcopy(xb.at[zz, c], xb.at[zz, c], c3s.at[zz], c3r.at[zz], core_mate)
 
     def cot_copy(i, src, b, dev):
         return rcopy(src, cb.at[b], cs.at[i], cr.at[b], dev)
@@ -168,12 +196,6 @@
         dx = jnp.where(q >= 6, q - 6, q // 3)
         return ((y + dy) % NY) * 2 + (xh + dx) % 2
 
-    def x2copy(zz):
-        return rcopy(xb.at[zz, c, xl], xb.at[zz, c, xl], x2s.at[zz], x2r.at[zz], x_mate)
-
-    def c3copy(zz):
-        return rcopy(xb.at[zz, c], xb.at[zz, c], c3s.at[zz], c3r.at[zz], core_mate)
-
     def pre_slot(dy, xx):
         return jnp.where(dy == 2, 4 + xx, jnp.where(dy == 1, xx, 2 + xx))
 
@@ -183,6 +205,14 @@
         yy = jnp.where(up, (y + 1) % NY, (y + NY - 1) % NY)
         return rcopy(ps.at[dy, xx], rb.at[slot], pss.at[slot], prs.at[slot], at_row(yy * 2 + xh))
 
+    def late(zz):
+        d = (zz - z + NZ) % NZ
+        return (d >= FAR_OFF) & (d <= NZ - FAR_OFF)
+
+    def direct_copy(zz):
+        dy, xx = (zz // 2 + NY - y) % NY, zz % 2
+        return rcopy(ps.at[dy, xx], rd.at[row], ds.at[zz], dr.at[row], at_row(zz))
+
     far_copy = rcopy(xsb, xrb, pxs, pxr, far_mate)
 
     def bccopy(b):
@@ -193,6 +223,10 @@
 
     def bzcopy(b):
         return rcopy(zsend.at[b], zrecv.at[z], bzs.at[b], bzr.at[z], at_col(b, xl, c))
+
+    z_add0, z_add1, z_far = ((y + 1) % NY) * 2, ((y + 3) % NY) * 2 + 1, y * 2 + 1 - xh
+    z_two0, z_two1 = ((y + 2) % NY) * 2, ((y + 2) % NY) * 2 + 1
+    z_dir1, z_dir3 = ((y + 1) % NY) * 2 + 1, ((y + 3) % NY) * 2
 
     def forward_block(zz):
         xs = jnp.concatenate([xb[zz, 0, 0], xb[zz, 1, 0], xb[zz, 0, 1], xb[zz, 1, 1]], axis=0)
@@ -205,7 +239,11 @@
         low = mm_nt(a_v[block_tenant(zz)], xs)
         lsend[zz] = low
 
-        @pl.when((dy == 2) | ((dy == 1) & (xx == 1)) | ((dy == 3) & (xx == 0)))
+        @pl.when(late(zz) & (zz != row))
+        def _():
+            direct_copy(zz).start()
+
+        @pl.when((~late(zz)) & ((dy == 2) | ((dy == 1) & (xx == 1)) | ((dy == 3) & (xx == 0))))
         def _():
             pre_copy(dy, xx).start()
 
@@ -241,32 +279,45 @@
         bccopy(b).start()
 
     def step(s, carry):
-        @pl.when(s < NZ)
-        def _():
-            zz = z_of(s)
-
-            @pl.when(s > 0)
+        for h, at in ((1, 0), (2, 2), (3, 4)):
+            @pl.when(s == at)
             def _():
-                got(xb.at[zz, c, xl], zr.at[zz])
-
-            x2copy(zz).start()
-
-        @pl.when((s >= 1) & (s < NZ + 1))
-        def _():
-            zz = z_of(s - 1)
-            got(xb.at[zz, c, 1 - xl], x2r.at[zz])
-            c3copy(zz).start()
-
-        @pl.when(s == 2)
+                for way in range(2):
+                    ring_got(way, h)
+                    ring(way, h).start()
+                for zz in ((z + NZ - h) % NZ, (z + h) % NZ):
+                    x2copy(zz).start()
+                for zz in ((z + NZ - h + 1) % NZ, (z + h - 1) % NZ)[: 1 if h == 1 else 2]:
+                    x2_got(zz)
+                    c3copy(zz).start()
+
+        @pl.when(s == 6)
+        def _():
+            ring_got(0, 4)
+            ring_got(1, 4)
+            x2copy((z + 4) % NZ).start()
+            for zz in ((z + NZ - 3) % NZ, (z + 3) % NZ):
+                x2_got(zz)
+                c3copy(zz).start()
+
+        @pl.when(s == 7)
+        def _():
+            x2_got((z + 4) % NZ)
+            c3copy((z + 4) % NZ).start()
+
+        @pl.when(s == AT_FAR)
         def _():
             got(cb.at[b_far], cr.at[b_far])
             cot_sends[3].start()
             cot_sends[4].start()
 
-        @pl.when(s == 4)
+        @pl.when(s == AT_DOWN)
         def _():
             got(cb.at[b_dn], cr.at[b_dn])
             cot_sends[5].start()
+
+        @pl.when(s == AT_NORM)
+        def _():
             for o in range(1, NR):
                 r = (row + o) % NR
                 got(nrecv.at[r], n1r.at[r])
@@ -280,37 +331,48 @@
             for o in range(1, NR):
                 n2copy(o).start()
 
-        @pl.when((s >= 2) & (s < NZ + 2))
-        def _():
-            zz = z_of(s - 2)
+        @pl.when((s == 1) | ((s >= 3) & (s < NZ + 2)))
+        def _():
+            zz = z_of(jnp.where(s == 1, 0, s - 2))
             got(xb.at[zz, 1 - c], c3r.at[zz])
             forward_block(zz)
 
-        @pl.when(s == FIRST_BACK)
+        @pl.when(s == AT_SCALE)
         def _():
             for o in range(1, NR):
                 r = (row + o) % NR
                 got(sbuf.at[r], n2r.at[r])
+
+        @pl.when(s == AT_UPFAR)
+        def _():
             got(cb.at[b_upfar], cr.at[b_upfar])
             cot_sends[6].start()
 
-        @pl.when(s == NZ + 2)
+        @pl.when((s == AT_VIA) & ~late(z_add0))
         def _():
             got(rb.at[4], prs.at[4])
             ps[1, 0] = (pf[1, 0] + rb[4].astype(F32)).astype(BF)
             pre_copy(1, 0).start()
+
+        @pl.when((s == AT_VIA) & ~late(z_add1))
+        def _():
             got(rb.at[5], prs.at[5])
             ps[3, 1] = (pf[3, 1] + rb[5].astype(F32)).astype(BF)
             pre_copy(3, 1).start()
 
-        @pl.when(s == NZ + 4)
+        @pl.when(s == AT_LOW)
         def _():
             for o in range(1, NR):
                 r = (row + o) % NR
                 got(lrecv.at[r], l1r.at[r])
-            lowb[row] = jnp.sum(lrecv[...], axis=0).astype(BF)
+            low = jnp.sum(lrecv[...], axis=0)
+            lowb[row] = low.astype(BF)
             for o in range(1, NR):
                 l2copy(o).start()
+            low_mine = low.astype(BF).astype(F32).T.astype(BF)
+            u_mine = u_v[block_tenant(row)]
+            for n0, n1 in lane_tiles(cols):
+                pf[0, xh, :, n0:n1] = pf[0, xh, :, n0:n1] + mm(low_mine, u_mine[:, n0:n1])
 
         @pl.when((s >= FIRST_BACK) & (s < FIRST_BACK + NR))
         def _():
@@ -323,17 +385,17 @@
 
             backward_block(b)
 
-        @pl.when((s >= FIRST_BACK + 1) & (s < FIRST_BACK + 1 + NR))
-        def _():
-            b = b_of(s - FIRST_BACK - 1)
+        @pl.when((s >= FIRST_BACK + LAG_X) & (s < FIRST_BACK + LAG_X + NR))
+        def _():
+            b = b_of(s - FIRST_BACK - LAG_X)
             got(crecv.at[b], bcr.at[b])
             xsend[b] = (gp[b, 1 - xl, c] + crecv[b, 1 - xl].astype(F32)).astype(BF)
             bxcopy(b).start()
             e_own[b] = gp[b, xl, c] + crecv[b, xl].astype(F32)
 
-        @pl.when(s >= FIRST_BACK + 2)
-        def _():
-            b = b_of(s - FIRST_BACK - 2)
+        @pl.when(s >= FIRST_BACK + LAG_Z)
+        def _():
+            b = b_of(s - FIRST_BACK - LAG_Z)
             got(xrecv.at[b], bxr.at[b])
             both = e_own[b] + xrecv[b].astype(F32)
             zsend[b] = both.astype(BF)
@@ -350,11 +412,28 @@
 
     lax.fori_loop(0, STEPS, step, 0)
 
-    for slot in range(4):
-        got(rb.at[slot], prs.at[slot])
-    xx = 1 - xh
-    xsb[...] = (pf[0, xx] + rb[xx].astype(F32) + rb[2 + xx].astype(F32)).astype(BF)
-    far_copy.start()
+    def magnitude_part(b, carry):
+        dy = (b // 2 + NY - y) % NY
+        part = jnp.sum(cb[b].astype(F32) * pf[dy, b % 2], axis=0, keepdims=True)
+        gms[row, b] = part * token_scale(b)
+        return carry
+
+    lax.fori_loop(0, NR, magnitude_part, 0)
+
+    def gcopy(o):
+        r = (row + o) % NR
+        return rcopy(gms.at[row], gms.at[row], gs.at[o], gr.at[row], at_row(r))
+
+    for o in range(1, NR):
+        gcopy(o).start()
+
+    @pl.when(~late(z_far))
+    def _():
+        xx = 1 - xh
+        got(rb.at[xx], prs.at[xx])
+        got(rb.at[2 + xx], prs.at[2 + xx])
+        xsb[...] = (pf[0, xx] + rb[xx].astype(F32) + rb[2 + xx].astype(F32)).astype(BF)
+        far_copy.start()
 
     for o in range(1, NR):
         r = (row + o) % NR
@@ -371,25 +450,6 @@
     gb_out = pltpu.make_async_copy(gb_v, gb_ref, gb_sem)
     gb_out.start()
 
-    got(xrb, pxr)
-    u_mine = u_v[block_tenant(row)]
-    low_mine = lowb[row].astype(F32).T.astype(BF)
-    scale_mine = token_scale(row)
-    for n0, n1 in lane_tiles(cols):
-        pre = pf[0, xh, :, n0:n1] + rb[xh, :, n0:n1].astype(F32) + rb[2 + xh, :, n0:n1].astype(F32)
-        pre = pre + xrb[:, n0:n1].astype(F32) + mm(low_mine, u_mine[:, n0:n1])
-        result = (pre * scale_mine[:, n0:n1]).astype(BF)
-        out_ref[:, n0:n1] = result
-        product = cb[row, :, n0:n1].astype(F32) * result.astype(F32)
-        gms[row, :, n0:n1] = jnp.sum(product, axis=0, keepdims=True)
-
-    def gcopy(o):
-        r = (row + o) % NR
-        return rcopy(gms.at[row], gms.at[row], gs.at[o], gr.at[row], at_row(r))
-
-    for o in range(1, NR):
-        gcopy(o).start()
-
     for o in range(1, NZ):
         zz = (z + o) % NZ
         got(zrecv.at[zz], bzr.at[zz])
@@ -398,19 +458,42 @@
         total = total + zrecv[(z + o) % NZ].astype(F32)
     gi_ref[...] = total.astype(BF)
 
+    scale_mine = token_scale(row)
+
+    @pl.when(late(row))
+    def _():
+        for o in range(1, NR):
+            r = (row + o) % NR
+            got(rd.at[r], dr.at[r])
+        for n0, n1 in lane_tiles(cols):
+            pre = pf[0, xh, :, n0:n1]
+            for o in range(1, NR):
+                pre = pre + rd[(row + o) % NR, :, n0:n1].astype(F32)
+            out_ref[:, n0:n1] = (pre * scale_mine[:, n0:n1]).astype(BF)
+
+    @pl.when(~late(row))
+    def _():
+        got(rb.at[xh], prs.at[xh])
+        got(rb.at[2 + xh], prs.at[2 + xh])
+        got(xrb, pxr)
+        for n0, n1 in lane_tiles(cols):
+            pre = pf[0, xh, :, n0:n1] + rb[xh, :, n0:n1].astype(F32) + rb[2 + xh, :, n0:n1].astype(F32)
+            pre = pre + xrb[:, n0:n1].astype(F32)
+            out_ref[:, n0:n1] = (pre * scale_mine[:, n0:n1]).astype(BF)
+
     for o in range(1, NR):
         r = (row + o) % NR
         got(gms.at[r], gr.at[r])
+    sums = jnp.sum(gms[...], axis=0)
     m = mag[...]
     number = lax.broadcasted_iota(jnp.int32, m.shape, 0)
     acc = jnp.zeros_like(m)
     for b in range(NR):
-        acc = acc + jnp.where(number == block_tenant(b), gms[b], 0.0)
+        acc = acc + jnp.where(number == block_tenant(b), sums[b], 0.0)
     gm_ref[...] = acc / m
 
     gb_out.wait()
     for o in range(1, NZ):
-        sent(x_in, zs.at[o])
         sent(nsend.at[0], n1s.at[o])
         sent(sbuf.at[0], n2s.at[o])
         sent(lowb.at[0], l2s.at[o])
@@ -430,9 +513,36 @@
             sent(lsend.at[k], l1s.at[k])
     for i in range(7):
         sent(c_in, cs.at[i])
-    for i in range(6):
-        sent(rb.at[i], pss.at[i])
-    sent(xsb, pxs)
+    for slot, zz in enumerate((z_add0, z_dir1, z_dir3, z_add1, z_two0, z_two1)):
+        @pl.when(~late(zz))
+        def _():
+            sent(rb.at[slot], pss.at[slot])
+
+    for zz in range(NR):
+        @pl.when(late(zz) & (zz != row))
+        def _():
+            sent(ps.at[0, 0], ds.at[zz])
+
+    @pl.when(~late(z_far))
+    def _():
+        sent(xsb, pxs)
+
+    for way in range(2):
+        for h in range(4):
+            sent(x_in if h < 3 else x_in.at[pl.ds(0, 16)], zs.at[way, h])
+
+
+def hand_over(*refs):
+    held, into, out = refs[8:12], refs[12], refs[13]
+    ins = [pltpu.make_async_copy(refs[i], held[i], into.at[i]) for i in range(4)]
+    outs = [pltpu.make_async_copy(held[i], refs[4 + i], out.at[i]) for i in range(4)]
+    for one in ins:
+        one.start()
+    for i in range(4):
+        ins[i].wait()
+        outs[i].start()
+    for one in outs:
+        one.wait()
 
 
 def shards(inputs, weight, adapter_down_factors, adapter_up_factors, magnitude, cotangent, tenant):
@@ -441,7 +551,7 @@
     any_, vmem = pl.BlockSpec(memory_space=pl.ANY), pl.BlockSpec(memory_space=pltpu.VMEM)
     dma = pltpu.SemaphoreType.DMA
     V = pltpu.VMEM
-    return pl.pallas_call(
+    parts = pl.pallas_call(
         kernel,
         out_shape=(
             jax.ShapeDtypeStruct((rows, cols), BF),
@@ -458,17 +568,17 @@
             V((NR, 2, cols), F32), V((NR, 2, cols), F32), V((NR, 2, cols), F32),
             V((NR, 16, rows), F32), V((NR, 16, rows), F32), V((NR, 16, rows), BF),
             V((NY, 2, rows, cols), F32), V((NY, 2, rows, cols), BF), V((6, rows, cols), BF),
-            V((rows, cols), BF), V((rows, cols), BF),
+            V((rows, cols), BF), V((rows, cols), BF), V((NR, rows, cols), BF),
             V((NR, 2, 2, tokens, width), F32), V((NR, 2, tokens, width), BF), V((NR, 2, tokens, width), BF),
             V((NR, tokens, width), F32),
             V((NR, tokens, width), BF), V((NR, tokens, width), BF),
             V((NR, tokens, width), BF), V((NR, tokens, width), BF),
-            V((NR, 1, cols), F32),
+            V((NR, NR, 1, cols), F32),
             dma((5,)), dma,
-            dma((8,)), dma((8,)), dma((8,)), dma((8,)), dma((8,)), dma((8,)),
+            dma((2, 4)), dma((8, 2)), dma((8,)), dma((8,)), dma((8,)), dma((8,)),
             dma((7,)), dma((8,)),
             dma((8,)), dma((8,)), dma((8,)), dma((8,)), dma((8,)), dma((8,)), dma((8,)), dma((8,)), dma((8,)), dma((8,)),
-            dma((6,)), dma((6,)), dma, dma,
+            dma((6,)), dma((6,)), dma, dma, dma((8,)), dma((8,)),
             dma((8,)), dma((8,)), dma((8,)), dma((8,)), dma((8,)), dma((8,)),
         ],
         compiler_params=pltpu.CompilerParams(
@@ -477,6 +587,14 @@
         cost_estimate=pl.CostEstimate(flops=6 * 10**9, bytes_accessed=8 * 10**6, transcendentals=10**5),
         name="adapter_step",
     )(tenant, inputs, weight, adapter_down_factors, adapter_up_factors, magnitude, cotangent)
+    return pl.pallas_call(
+        hand_over,
+        out_shape=[jax.ShapeDtypeStruct(p.shape, p.dtype) for p in parts],
+        in_specs=[any_] * 4,
+        out_specs=[any_] * 4,
+        scratch_shapes=[V(p.shape, p.dtype) for p in parts] + [dma((4,)), dma((4,))],
+        name="hand_over",
+    )(*parts)
 
 
 def solution(mesh):

time: 92.9 us -> 68.3 us (0.74)
  the two profiles are of different devices: /device:TPU:32 before, /device:TPU:1 now
where the time goes in v2:
time: 68.3 us; the launch traced here: 68 us
  Pallas kernels  67.4 us (99%)
    pallas_call x1, Pallas kernels, shards(): pl.pallas_call(kernel, out_shape=(jax.ShapeDtypeStruct((rows, cols), BF),...  65.1 us
    pallas_call x1, Pallas kernels, shards(): pl.pallas_call(hand_over, out_shape=[jax.ShapeDtypeStruct(p.shape, p.dtyp...  2.33 us

profile of v2, /device:TPU:1, one launch (start us, length us, event | category | flops | bytes accessed | tf_op | source)
XLA Modules:
  0.0 68.0 jit_solution(7711376013880535212)
XLA Ops:
  0.6 65.1 %adapter_step.1 = (bf16[128,896]{1,0:T(8,128)(2,1)}, bf16[32,1024]{1,0:T(8,128)(2,1)}, f32[16,16,896]{2,1,0:T(8,128)}, f32[16,896]{1,0:T(8,128)}) custom-call(s32[1024]{0:T(1024)} %ten.1, bf16[32,1024]{1,0:T(8,128)(2,1)} %x_in.1, bf16[1024,896]{1,0:T(8,128)(2,1)} %w_in.1, bf16[16,16,1024]{2,1,0:T(8,128)(2,1)} %a_in.1, bf16[16,16,896]{2,1,0:T(8,128)(2,1)} %u_in.1, ...), custom_call_target="tpu_custom_call" | custom-call | flops 6000000000 | bytes 8000000 | tf_op jit(solution)/shard_map/adapter_step/pallas_call | solution.py:554
  65.7 2.3 %hand_over.1 = (bf16[128,896]{1,0:T(8,128)(2,1)}, bf16[32,1024]{1,0:T(8,128)(2,1)}, f32[16,16,896]{2,1,0:T(8,128)}, f32[16,896]{1,0:T(8,128)}) custom-call(bf16[128,896]{1,0:T(8,128)(2,1)} %get-tuple-element.8.refs_0_, bf16[32,1024]{1,0:T(8,128)(2,1)} %get-tuple-element.9.refs_1_, f32[16,16,896]{2,1,0:T(8,128)} %get-tuple-element.10.refs_2_, ...), custom_call_target="tpu_custom_call" | custom-call | tf_op jit(solution)/shard_map/hand_over/pallas_call | solution.py:590

commit v3 on v2

--- a/solution.py
+++ b/solution.py
@@ -14,9 +14,8 @@
 
 NZ, NY, NR = 8, 4, 8
 AT_FAR, AT_DOWN, AT_UPFAR = 2, 2, 6
-AT_NORM, AT_SCALE, AT_VIA, AT_LOW = 1, 5, 13, 13
-FIRST_BACK, LAG_X, LAG_Z = 5, 2, 4
-FAR_OFF = 5
+AT_NORM, AT_SCALE, AT_VIA, AT_LOW = 1, 4, 12, 14
+FIRST_BACK, LAG_X, LAG_Z = 4, 2, 4
 STEPS = FIRST_BACK + NZ + LAG_Z
 
 
@@ -38,14 +37,14 @@
     w_v, a_v, u_v, xb, cb, sgb, gb_v,
     nsend, nrecv, sbuf,
     lsend, lrecv, lowb,
-    pf, ps, rb, xsb, xrb, rd,
+    pf, ps, rb, xsb, xrb,
     gp, csend, crecv, e_own, xsend, xrecv, zsend, zrecv,
     gms,
     loc_sem, gb_sem,
     zs, zr, x2s, x2r, c3s, c3r,
     cs, cr,
     n1s, n1r, n2s, n2r, l1s, l1r, l2s, l2r, gs, gr,
-    pss, prs, pxs, pxr, ds, dr,
+    pss, prs, pxs, pxr,
     bcs, bcr, bxs, bxr, bzs, bzr,
 ):
     col = lax.axis_index("col")
@@ -199,21 +198,21 @@
     def pre_slot(dy, xx):
         return jnp.where(dy == 2, 4 + xx, jnp.where(dy == 1, xx, 2 + xx))
 
-    def pre_copy(dy, xx):
+    def pre_copy(dy, xx, half):
         slot = pre_slot(dy, xx)
         up = (dy == 1) | ((dy == 2) & (xx == 0))
         yy = jnp.where(up, (y + 1) % NY, (y + NY - 1) % NY)
-        return rcopy(ps.at[dy, xx], rb.at[slot], pss.at[slot], prs.at[slot], at_row(yy * 2 + xh))
-
-    def late(zz):
-        d = (zz - z + NZ) % NZ
-        return (d >= FAR_OFF) & (d <= NZ - FAR_OFF)
-
-    def direct_copy(zz):
-        dy, xx = (zz // 2 + NY - y) % NY, zz % 2
-        return rcopy(ps.at[dy, xx], rd.at[row], ds.at[zz], dr.at[row], at_row(zz))
-
-    far_copy = rcopy(xsb, xrb, pxs, pxr, far_mate)
+        part = pl.ds(64 * half, 64)
+        return rcopy(
+            ps.at[dy, xx, part], rb.at[slot, part], pss.at[slot, half], prs.at[slot, half], at_row(yy * 2 + xh)
+        )
+
+    def pre_got(slot, half):
+        got(rb.at[slot, pl.ds(64 * half, 64)], prs.at[slot, half])
+
+    def far_copy(half):
+        part = pl.ds(64 * half, 64)
+        return rcopy(xsb.at[part], xrb.at[part], pxs.at[half], pxr.at[half], far_mate)
 
     def bccopy(b):
         return rcopy(csend.at[b], crecv.at[b], bcs.at[b], bcr.at[b], core_mate)
@@ -223,10 +222,6 @@
 
     def bzcopy(b):
         return rcopy(zsend.at[b], zrecv.at[z], bzs.at[b], bzr.at[z], at_col(b, xl, c))
-
-    z_add0, z_add1, z_far = ((y + 1) % NY) * 2, ((y + 3) % NY) * 2 + 1, y * 2 + 1 - xh
-    z_two0, z_two1 = ((y + 2) % NY) * 2, ((y + 2) % NY) * 2 + 1
-    z_dir1, z_dir3 = ((y + 1) % NY) * 2 + 1, ((y + 3) % NY) * 2
 
     def forward_block(zz):
         xs = jnp.concatenate([xb[zz, 0, 0], xb[zz, 1, 0], xb[zz, 0, 1], xb[zz, 1, 1]], axis=0)
@@ -239,13 +234,10 @@
         low = mm_nt(a_v[block_tenant(zz)], xs)
         lsend[zz] = low
 
-        @pl.when(late(zz) & (zz != row))
-        def _():
-            direct_copy(zz).start()
-
-        @pl.when((~late(zz)) & ((dy == 2) | ((dy == 1) & (xx == 1)) | ((dy == 3) & (xx == 0))))
-        def _():
-            pre_copy(dy, xx).start()
+        @pl.when((dy == 2) | ((dy == 1) & (xx == 1)) | ((dy == 3) & (xx == 0)))
+        def _():
+            for half in range(2):
+                pre_copy(dy, xx, half).start()
 
         @pl.when(zz != row)
         def _():
@@ -348,18 +340,6 @@
             got(cb.at[b_upfar], cr.at[b_upfar])
             cot_sends[6].start()
 
-        @pl.when((s == AT_VIA) & ~late(z_add0))
-        def _():
-            got(rb.at[4], prs.at[4])
-            ps[1, 0] = (pf[1, 0] + rb[4].astype(F32)).astype(BF)
-            pre_copy(1, 0).start()
-
-        @pl.when((s == AT_VIA) & ~late(z_add1))
-        def _():
-            got(rb.at[5], prs.at[5])
-            ps[3, 1] = (pf[3, 1] + rb[5].astype(F32)).astype(BF)
-            pre_copy(3, 1).start()
-
         @pl.when(s == AT_LOW)
         def _():
             for o in range(1, NR):
@@ -408,6 +388,15 @@
             def _():
                 e_own[b] = both
 
+        @pl.when(s == AT_VIA)
+        def _():
+            for half in range(2):
+                rows = pl.ds(64 * half, 64)
+                for slot, dy, xx in ((4, 1, 0), (5, 3, 1)):
+                    pre_got(slot, half)
+                    ps[dy, xx, rows] = (pf[dy, xx, rows] + rb[slot, rows].astype(F32)).astype(BF)
+                    pre_copy(dy, xx, half).start()
+
         return carry
 
     lax.fori_loop(0, STEPS, step, 0)
@@ -427,13 +416,13 @@
     for o in range(1, NR):
         gcopy(o).start()
 
-    @pl.when(~late(z_far))
-    def _():
-        xx = 1 - xh
-        got(rb.at[xx], prs.at[xx])
-        got(rb.at[2 + xx], prs.at[2 + xx])
-        xsb[...] = (pf[0, xx] + rb[xx].astype(F32) + rb[2 + xx].astype(F32)).astype(BF)
-        far_copy.start()
+    xx = 1 - xh
+    for half in range(2):
+        rows = pl.ds(64 * half, 64)
+        pre_got(xx, half)
+        pre_got(2 + xx, half)
+        xsb[rows] = (pf[0, xx, rows] + rb[xx, rows].astype(F32) + rb[2 + xx, rows].astype(F32)).astype(BF)
+        far_copy(half).start()
 
     for o in range(1, NR):
         r = (row + o) % NR
@@ -460,26 +449,15 @@
 
     scale_mine = token_scale(row)
 
-    @pl.when(late(row))
-    def _():
-        for o in range(1, NR):
-            r = (row + o) % NR
-            got(rd.at[r], dr.at[r])
+    for half in range(2):
+        rows = pl.ds(64 * half, 64)
+        pre_got(xh, half)
+        pre_got(2 + xh, half)
+        got(xrb.at[rows], pxr.at[half])
         for n0, n1 in lane_tiles(cols):
-            pre = pf[0, xh, :, n0:n1]
-            for o in range(1, NR):
-                pre = pre + rd[(row + o) % NR, :, n0:n1].astype(F32)
-            out_ref[:, n0:n1] = (pre * scale_mine[:, n0:n1]).astype(BF)
-
-    @pl.when(~late(row))
-    def _():
-        got(rb.at[xh], prs.at[xh])
-        got(rb.at[2 + xh], prs.at[2 + xh])
-        got(xrb, pxr)
-        for n0, n1 in lane_tiles(cols):
-            pre = pf[0, xh, :, n0:n1] + rb[xh, :, n0:n1].astype(F32) + rb[2 + xh, :, n0:n1].astype(F32)
-            pre = pre + xrb[:, n0:n1].astype(F32)
-            out_ref[:, n0:n1] = (pre * scale_mine[:, n0:n1]).astype(BF)
+            pre = pf[0, xh, rows, n0:n1] + rb[xh, rows, n0:n1].astype(F32) + rb[2 + xh, rows, n0:n1].astype(F32)
+            pre = pre + xrb[rows, n0:n1].astype(F32)
+            out_ref[rows, n0:n1] = (pre * scale_mine[:, n0:n1]).astype(BF)
 
     for o in range(1, NR):
         r = (row + o) % NR
@@ -513,20 +491,11 @@
             sent(lsend.at[k], l1s.at[k])
     for i in range(7):
         sent(c_in, cs.at[i])
-    for slot, zz in enumerate((z_add0, z_dir1, z_dir3, z_add1, z_two0, z_two1)):
-        @pl.when(~late(zz))
-        def _():
-            sent(rb.at[slot], pss.at[slot])
-
-    for zz in range(NR):
-        @pl.when(late(zz) & (zz != row))
-        def _():
-            sent(ps.at[0, 0], ds.at[zz])
-
-    @pl.when(~late(z_far))
-    def _():
-        sent(xsb, pxs)
-
+    for half in range(2):
+        rows = pl.ds(64 * half, 64)
+        for slot in range(6):
+            sent(rb.at[slot, rows], pss.at[slot, half])
+        sent(xsb.at[rows], pxs.at[half])
     for way in range(2):
         for h in range(4):
             sent(x_in if h < 3 else x_in.at[pl.ds(0, 16)], zs.at[way, h])
@@ -568,7 +537,7 @@
             V((NR, 2, cols), F32), V((NR, 2, cols), F32), V((NR, 2, cols), F32),
             V((NR, 16, rows), F32), V((NR, 16, rows), F32), V((NR, 16, rows), BF),
             V((NY, 2, rows, cols), F32), V((NY, 2, rows, cols), BF), V((6, rows, cols), BF),
-            V((rows, cols), BF), V((rows, cols), BF), V((NR, rows, cols), BF),
+            V((rows, cols), BF), V((rows, cols), BF),
             V((NR, 2, 2, tokens, width), F32), V((NR, 2, tokens, width), BF), V((NR, 2, tokens, width), BF),
             V((NR, tokens, width), F32),
             V((NR, tokens, width), BF), V((NR, tokens, width), BF),
@@ -578,7 +547,7 @@
             dma((2, 4)), dma((8, 2)), dma((8,)), dma((8,)), dma((8,)), dma((8,)),
             dma((7,)), dma((8,)),
             dma((8,)), dma((8,)), dma((8,)), dma((8,)), dma((8,)), dma((8,)), dma((8,)), dma((8,)), dma((8,)), dma((8,)),
-            dma((6,)), dma((6,)), dma, dma, dma((8,)), dma((8,)),
+            dma((6, 2)), dma((6, 2)), dma((2,)), dma((2,)),
             dma((8,)), dma((8,)), dma((8,)), dma((8,)), dma((8,)), dma((8,)),
         ],
         compiler_params=pltpu.CompilerParams(

time: 68.3 us -> 66.8 us (0.978)
  Pallas kernels: 67.4 us -> 65.9 us
    pallas_call x1, Pallas kernels: 65.1 us -> 63.6 us  [shards(): pl.pallas_call(kernel, out_shape=(jax.ShapeDtypeStruct((rows, cols), BF),...]
where the time goes in v3:
time: 66.8 us; the launch traced here: 66.6 us
  Pallas kernels  65.9 us (99%)
    pallas_call x1, Pallas kernels, shards(): pl.pallas_call(kernel, out_shape=(jax.ShapeDtypeStruct((rows, cols), BF),...  63.6 us
    pallas_call x1, Pallas kernels, shards(): pl.pallas_call(hand_over, out_shape=[jax.ShapeDtypeStruct(p.shape, p.dtyp...  2.33 us

profile of v3, /device:TPU:1, one launch (start us, length us, event | category | flops | bytes accessed | tf_op | source)
XLA Modules:
  0.0 66.6 jit_solution(16009186051535781141)
XLA Ops:
  0.6 63.6 %adapter_step.1 = (bf16[128,896]{1,0:T(8,128)(2,1)}, bf16[32,1024]{1,0:T(8,128)(2,1)}, f32[16,16,896]{2,1,0:T(8,128)}, f32[16,896]{1,0:T(8,128)}) custom-call(s32[1024]{0:T(1024)} %ten.1, bf16[32,1024]{1,0:T(8,128)(2,1)} %x_in.1, bf16[1024,896]{1,0:T(8,128)(2,1)} %w_in.1, bf16[16,16,1024]{2,1,0:T(8,128)(2,1)} %a_in.1, bf16[16,16,896]{2,1,0:T(8,128)(2,1)} %u_in.1, ...), custom_call_target="tpu_custom_call" | custom-call | flops 6000000000 | bytes 8000000 | tf_op jit(solution)/shard_map/adapter_step/pallas_call | solution.py:523
  64.2 2.3 %hand_over.1 = (bf16[128,896]{1,0:T(8,128)(2,1)}, bf16[32,1024]{1,0:T(8,128)(2,1)}, f32[16,16,896]{2,1,0:T(8,128)}, f32[16,896]{1,0:T(8,128)}) custom-call(bf16[128,896]{1,0:T(8,128)(2,1)} %get-tuple-element.8.refs_0_, bf16[32,1024]{1,0:T(8,128)(2,1)} %get-tuple-element.9.refs_1_, f32[16,16,896]{2,1,0:T(8,128)} %get-tuple-element.10.refs_2_, ...), custom_call_target="tpu_custom_call" | custom-call | tf_op jit(solution)/shard_map/hand_over/pallas_call | solution.py:559

commit v4 on v3

--- a/solution.py
+++ b/solution.py
@@ -146,8 +146,7 @@
         cot_copy(5, cb.at[b_dn], b_dn, y_up),
         cot_copy(6, cb.at[b_upfar], b_upfar, y_down),
     ]
-    for one in cot_sends[:3]:
-        one.start()
+    cot_sends[0].start()
 
     for one in loads:
         one.wait()
@@ -175,6 +174,8 @@
 
     for o in range(1, NR):
         n1copy(o).start()
+    for one in cot_sends[1:3]:
+        one.start()
 
     def n2copy(o):
         r = (row + o) % NR

time: 66.8 us -> 66.8 us (level)
  no operation moved by 1% of the time
where the time goes in v4:
time: 66.8 us; the launch traced here: 66.6 us
  Pallas kernels  65.9 us (99%)
    pallas_call x1, Pallas kernels, shards(): pl.pallas_call(kernel, out_shape=(jax.ShapeDtypeStruct((rows, cols), BF),...  63.6 us
    pallas_call x1, Pallas kernels, shards(): pl.pallas_call(hand_over, out_shape=[jax.ShapeDtypeStruct(p.shape, p.dtyp...  2.33 us

profile of v4, /device:TPU:1, one launch (start us, length us, event | category | flops | bytes accessed | tf_op | source)
XLA Modules:
  0.0 66.6 jit_solution(16490190515768566761)
XLA Ops:
  0.6 63.6 %adapter_step.1 = (bf16[128,896]{1,0:T(8,128)(2,1)}, bf16[32,1024]{1,0:T(8,128)(2,1)}, f32[16,16,896]{2,1,0:T(8,128)}, f32[16,896]{1,0:T(8,128)}) custom-call(s32[1024]{0:T(1024)} %ten.1, bf16[32,1024]{1,0:T(8,128)(2,1)} %x_in.1, bf16[1024,896]{1,0:T(8,128)(2,1)} %w_in.1, bf16[16,16,1024]{2,1,0:T(8,128)(2,1)} %a_in.1, bf16[16,16,896]{2,1,0:T(8,128)(2,1)} %u_in.1, ...), custom_call_target="tpu_custom_call" | custom-call | flops 6000000000 | bytes 8000000 | tf_op jit(solution)/shard_map/adapter_step/pallas_call | solution.py:524
  64.2 2.3 %hand_over.1 = (bf16[128,896]{1,0:T(8,128)(2,1)}, bf16[32,1024]{1,0:T(8,128)(2,1)}, f32[16,16,896]{2,1,0:T(8,128)}, f32[16,896]{1,0:T(8,128)}) custom-call(bf16[128,896]{1,0:T(8,128)(2,1)} %get-tuple-element.8.refs_0_, bf16[32,1024]{1,0:T(8,128)(2,1)} %get-tuple-element.9.refs_1_, f32[16,16,896]{2,1,0:T(8,128)} %get-tuple-element.10.refs_2_, ...), custom_call_target="tpu_custom_call" | custom-call | tf_op jit(solution)/shard_map/hand_over/pallas_call | solution.py:560
